TPU v7x, 32 devices: a whole 2x2x4 slice. The times are simulated.
32 devices in a mesh: grp: 2 (over y), frm: 4 (over z), head: 2 (over x), pos: 2 (over core).
Axes of the slice: x: 2, y: 2, z: 4, core: 2. Of those that a mesh axis runs over, the one named last changes fastest.
Arguments:
- queries: float32 [32, 128, 3072], P(('grp', 'frm'), 'pos', 'head'), parts along dimension 0, may hold values from -120 to 120
- key_states: float32 [32, 128, 3072], P(('grp', 'frm'), 'pos', 'head'), parts along dimension 0, may hold values from -4 to 4
- value_states: float32 [32, 128, 3072], P(('grp', 'frm'), 'pos', 'head'), parts along dimension 0, may hold values from -6 to 6
- windows: int32 [24], P('head'), may hold values from 1 to 2, as said below
- strides: int32 [24], P('head'), may hold values from 4 to 8, as said below
- cutoffs: int32 [24], P('head'), may hold values from 1 to 2, as said below
Outputs:
- blended: float32 [32, 128, 3072], P(('grp', 'frm'), 'pos', 'head'), parts along dimension 0
There are 2 independent parts, one for each index of `grp`. A program takes and returns all parts, laid end to end along the dimension named above; an argument that names none is the same for every part. Nothing has to cross between parts.
Inputs may be any that keep to these rules, and one draw needn't show every extreme that they name: `windows`: some head has exactly 2. `strides`: each is 4 or 8, and both occur. `cutoffs`: some head has exactly 2.
All inputs are finite; a program needn't handle non-finite values.
Results may differ from a plain program's by a relative error of at most 0.0003.
Values sent between devices are 32-bit elements; how exact they have to be, the bound alone decides.
A program may use at most 128 MiB of HBM per device.

v0:
```python
import math

import jax
import jax.numpy as jnp
from jax import lax
from jax.sharding import PartitionSpec as P

DH = 128
KSTRIDE = 4


def with_halo(value, sides, width):
    for axis, dim in sides:
        size, length = (lax.axis_size(axis), value.shape[dim])
        up = [(i, (i + 1) % size) for i in range(size - 1)]
        down = [(j, i) for i, j in up]
        last = lax.slice_in_dim(value, length - width, length, axis=dim)
        first = lax.slice_in_dim(value, 0, width, axis=dim)
        before = lax.ppermute(last, axis, up)
        after = lax.ppermute(first, axis, down)
        value = jnp.concatenate([before, value, after], axis=dim)
    return value


def attend(query_rows, key_rows, value_rows, allowed, score_scale):
    scores = (
        jnp.einsum("qhd,khd->hqk", query_rows, key_rows, precision=lax.Precision.HIGHEST)
        * score_scale
    )
    highest = jnp.max(jnp.where(allowed, scores, -1e30), axis=2, keepdims=True)
    weights = jnp.where(allowed, jnp.exp(scores - highest), 0.0)
    row_total = jnp.sum(weights, axis=2, keepdims=True)
    return jnp.einsum(
        "hqk,khd->qhd", weights / row_total, value_rows, precision=lax.Precision.HIGHEST
    )


def shards(queries, key_states, value_states, windows, strides, cutoffs):
    frames_dev, half_tokens, channels = queries.shape
    heads_local = channels // DH
    frame_groups = lax.axis_size("frm")
    pos_count = lax.axis_size("pos")
    total_frames = frames_dev * frame_groups
    halo_frames = frames_dev // 2
    score_scale = DH ** (-0.5)
    query_count = frames_dev * half_tokens
    query_rows = queries.reshape(query_count, heads_local, DH)
    query_blocks = queries.reshape(frames_dev, half_tokens, heads_local, DH)
    first_frame = lax.axis_index("frm") * frames_dev
    key_full, value_full = (
        lax.all_gather(key_states, "pos", axis=1, tiled=True),
        lax.all_gather(value_states, "pos", axis=1, tiled=True),
    )
    full_tokens = key_full.shape[1]
    stacked = jnp.stack([key_full, value_full])
    padded = with_halo(stacked, (("frm", 1),), halo_frames)
    window_span = 2 * halo_frames + 1
    span_rows = window_span * full_tokens
    span_offsets = jnp.arange(span_rows, dtype=jnp.int32) // full_tokens - halo_frames

    def local_frame(frame_local):
        query_part = lax.dynamic_index_in_dim(query_blocks, frame_local, 0, keepdims=False)
        block = lax.dynamic_slice_in_dim(padded, frame_local, window_span, 1)
        near_keys = block[0].reshape(span_rows, heads_local, DH)
        near_values = block[1].reshape(span_rows, heads_local, DH)
        near_frames = first_frame + frame_local + span_offsets
        inside = (near_frames >= 0) & (near_frames < total_frames)
        allowed = inside[None, None, :] & (
            jnp.abs(span_offsets)[None, None, :] <= windows[:, None, None]
        )
        return attend(query_part, near_keys, near_values, allowed, score_scale)

    local_out = lax.map(local_frame, jnp.arange(frames_dev, dtype=jnp.int32)).reshape(
        query_count, heads_local, DH
    )
    frame_keys = key_states[::KSTRIDE].reshape(-1, heads_local, DH)
    frame_values = value_states[::KSTRIDE].reshape(-1, heads_local, DH)
    rows_dev = frame_keys.shape[0]
    key_part = lax.all_gather(frame_keys, ("frm", "pos"), axis=0, tiled=True)
    value_part = lax.all_gather(frame_values, ("frm", "pos"), axis=0, tiled=True)
    row_count = key_part.shape[0]
    row_ids = jnp.arange(row_count, dtype=jnp.int32)
    frame_ids = (
        row_ids // rows_dev // pos_count * frames_dev + row_ids % rows_dev // half_tokens * KSTRIDE
    )
    allowed = (frame_ids[None, :] % strides[:, None] == 0)[:, None, :]
    scores = (
        jnp.einsum("qhd,khd->hqk", query_rows, key_part, precision=lax.Precision.HIGHEST)
        * score_scale
    )
    top_old = jnp.full((heads_local, query_count), -1e30, jnp.float32)
    top_new = jnp.maximum(top_old, jnp.max(jnp.where(allowed, scores, -1e30), axis=2))
    weights = jnp.where(allowed, jnp.exp(scores - top_new[:, :, None]), 0.0)
    total_new = jnp.sum(weights, axis=2)
    accum_new = jnp.einsum("hqk,khd->hqd", weights, value_part, precision=lax.Precision.HIGHEST)
    final_state = (top_new, total_new, accum_new)
    top_final, total_final, accum_final = final_state
    global_out = jnp.transpose(accum_final / total_final[:, :, None], (1, 0, 2))
    frequency = jnp.arange(total_frames, dtype=jnp.int32)
    phase_index = frequency[:, None] * frequency[None, :] % total_frames
    phases = 2.0 * math.pi / total_frames * phase_index.astype(jnp.float32)
    cos_table = jnp.cos(phases)
    sin_table = jnp.sin(phases)
    distance_freq = jnp.minimum(frequency, total_frames - frequency)
    low_keep = (distance_freq[None, :] <= cutoffs[:, None]).astype(jnp.float32)
    lowpass = (
        jnp.einsum("kf,hk,kg->hfg", cos_table, low_keep, cos_table, precision=lax.Precision.HIGHEST)
        + jnp.einsum(
            "kf,hk,kg->hfg", sin_table, low_keep, sin_table, precision=lax.Precision.HIGHEST
        )
    ) / total_frames
    group_items = half_tokens // frame_groups
    local_grid = local_out.reshape(frames_dev, frame_groups, group_items, channels)
    global_grid = global_out.reshape(frames_dev, frame_groups, group_items, channels)
    frame_block = lax.all_to_all(
        global_grid - local_grid, "frm", split_axis=1, concat_axis=0, tiled=True
    )
    frames_all = frame_block.shape[0]
    item_count = frame_block.shape[2]
    shaped = frame_block.reshape(frames_all, item_count, heads_local, DH)
    filtered_block = jnp.einsum(
        "hfg,gihd->fihd", lowpass, shaped, precision=lax.Precision.HIGHEST
    ).reshape(frame_block.shape)
    filtered = lax.all_to_all(filtered_block, "frm", split_axis=0, concat_axis=1, tiled=True)
    blended = local_grid + filtered
    return blended.reshape(frames_dev, half_tokens, channels)


def solution(mesh):
    in_specs = (
        P(("grp", "frm"), "pos", "head"),
        P(("grp", "frm"), "pos", "head"),
        P(("grp", "frm"), "pos", "head"),
        P("head"),
        P("head"),
        P("head"),
    )
    out_specs = P(("grp", "frm"), "pos", "head")
    return jax.shard_map(shards, mesh=mesh, in_specs=in_specs, out_specs=out_specs, check_vma=False)
```

profile of v0, /device:TPU:0, one launch (start us, length us, event | category | flops | bytes accessed | tf_op | source)
XLA Modules:
  0.0 456.6 jit_solution(4020904043118848614)
XLA Ops:
  12.1 11.6 %all-gather.5.cloned.1.call-done = f32[4,128,1536]{2,1,0:T(8,128)} async-done(((f32[4,64,1536]{2,1,0:T(8,128)}), f32[4,128,1536]{2,1,0:T(8,128)}) %all-gather.5.cloned.1.call-update) | async-done | bytes 3145744 | tf_op jit(solution)/shard_map/all_gather | solution.py:51
  23.8 14.9 %all-gather.7.cloned.1.call-done = f32[4,128,1536]{2,1,0:T(8,128)} async-done(((f32[4,64,1536]{2,1,0:T(8,128)}), f32[4,128,1536]{2,1,0:T(8,128)}) %all-gather.7.cloned.1.call-update) | async-done | bytes 3145744 | tf_op jit(solution)/shard_map/all_gather | solution.py:52
  38.6 5.9 %fusion.46 = (f32[2,2,128,1536]{3,2,1,0:T(8,128)}, f32[2,2,128,1536]{3,2,1,0:T(8,128)}) fusion(f32[1,4,128,1536]{3,2,1,0:T(8,128)} %bitcast.70, f32[1,4,128,1536]{3,2,1,0:T(8,128)} %bitcast.72), kind=kLoop, calls=%fused_computation.52 | loop fusion | flops 1572864 | bytes 12582912 | tf_op jit(solution)/shard_map/stack | solution.py:55
  56.2 44.0 %all-gather.9.cloned.1.call-done = f32[512,12,128]{2,0,1:T(8,128)} async-done(((f32[64,12,128]{2,0,1:T(8,128)}), f32[512,12,128]{2,0,1:T(8,128)}) %all-gather.9.cloned.1.call-update) | async-done | bytes 3145744 | tf_op jit(solution)/shard_map/all_gather | solution.py:79
  100.2 7.8 %select_reduce_fusion.1 = (f32[12,256]{1,0:T(8,128)S(1)}, f32[12,256,512]{2,1,0:T(8,128)S(1)}) fusion(pred[12,512]{1,0:T(8,128)(4,1)S(1)} %fusion.69, f32[512,12,128]{2,0,1:T(8,128)} %all-gather.9.cloned.1.call-done, f32[256,12,128]{2,1,0:T(8,128)S(1)} %reshape.230), kind=kOutput, calls=%fused_computation.49 | convolution fusion | flops 2420634624 | bytes 11028480 | tf_op jit(solution)/shard_map/qhd,khd->hqk/dot_general | solution.py:88
  112.3 50.7 %all-gather.11.cloned.1.call-done = f32[512,12,128]{2,0,1:T(8,128)} async-done(((f32[64,12,128]{2,0,1:T(8,128)}), f32[512,12,128]{2,0,1:T(8,128)}) %all-gather.11.cloned.1.call-update) | async-done | bytes 3145744 | tf_op jit(solution)/shard_map/all_gather | solution.py:80
  163.0 10.8 %bitcast_divide_fusion = f32[256,12,128]{2,0,1:T(8,128)S(1)} fusion(f32[512,12,128]{2,0,1:T(8,128)} %all-gather.11.cloned.1.call-done, f32[12,256,512]{2,1,0:T(8,128)} %copy-done, f32[12,256]{1,0:T(8,128)S(1)} %broadcast_maximum_fusion, pred[12,512]{1,0:T(8,128)(4,1)S(1)} %fusion.69, f32[256,12]{0,1:T(8,128)S(1)} %bitcast.78), kind=kOutput, calls=%fused_computation.60 | convolution fusion | flops 2421030912 | bytes 11040768 | tf_op jit(solution)/shard_map/hqk,khd->hqd/dot_general | solution.py:95
  178.9 9.5 %pad_maximum_fusion = f32[2,8,128,1536]{3,2,1,0:T(8,128)} fusion(f32[2,2,128,1536]{3,2,1,0:T(8,128)} %collective-permute-done.1, f32[1,4,128,1536]{3,2,1,0:T(8,128)} %bitcast.73, f32[1,4,128,1536]{3,2,1,0:T(8,128)S(1)} %bitcast.71, f32[2,2,128,1536]{3,2,1,0:T(8,128)} %collective-permute-done), kind=kLoop, calls=%fused_computation.45 | loop fusion | flops 9437184 | bytes 25165824 | tf_op jit(solution)/shard_map/concatenate | solution.py:21
  188.5 159.4 %while.12 = (s32[]{:T(128)}, f32[4,64,12,128]{3,1,2,0:T(8,128)}, s32[4]{0:T(128)S(1)}, f32[2,8,128,1536]{3,2,1,0:T(8,128)}, s32[]{:T(128)}, /*index=5*/s32[12]{0...) while((s32[]{:T(128)}, f32[4,64,12,128]{3,1,2,0:T(8,128)}, ...), condition=%wide.region_3.4_spmd.clone, body=%wide.region_0.3_spmd.clone.sunk | while | flops 1513420800 | bytes 58486832 | solution.py:73
  190.7 7.1 %constant_dynamic-slice_fusion.3 = (f32[1,5,128,1536]{3,2,1,0:T(8,128)}, f32[1,5,128,1536]{3,2,1,0:T(8,128)}) fusion(f32[2,8,128,1536]{3,2,1,0:T(8,128)} %get-tuple-element.216, s32[]{:T(128)S(6)} %add.172, s32[]{:T(128)S(6)} %select_n.212), kind=kLoop, calls=%fused_computation.41.clone.1 | loop fusion | bytes 15728648 | tf_op jit(solution)/shard_map/while/body/eval_jaxpr/slice | solution.py:65
  204.2 8.7 %fusion.129 = f32[12,64,640]{2,1,0:T(8,128)S(1)} fusion(f32[640,12,128]{2,1,0:T(8,128)} %squeeze.24, f32[4,64,12,128]{3,1,2,0:T(8,128)} %get-tuple-element.219, s32[]{:T(128)S(6)} %select_n.213), kind=kOutput, calls=%fused_computation.5.clone.1 | convolution fusion | flops 754974720 | bytes 7602180 | tf_op jit(solution)/shard_map/while/body/eval_jaxpr/qhd,khd->hqk/dot_general | solution.py:27
  221.1 7.3 %fusion.133 = f32[4,64,12,128]{3,1,2,0:T(8,128)} fusion(f32[4,64,12,128]{3,1,2,0:T(8,128)} %get-tuple-element.202, s32[]{:T(128)} %get-tuple-element.201, f32[12,64,640]{2,1,0:T(8,128)S(1)} %copy-done.7, f32[640,12,128]{2,1,0:T(8,128)} %squeeze.25, f32[12,64]{1,0:T(8,128)S(1)} %get-tuple-element.188), kind=kOutput, calls=%fused_computation.13.clone.1 | convolution fusion | flops 755466240 | bytes 7605760 | tf_op jit(solution)/shard_map/while/body/eval_jaxpr/hqk,khd->qhd/dot_general | solution.py:33
  230.5 7.1 %constant_dynamic-slice_fusion.3 = (f32[1,5,128,1536]{3,2,1,0:T(8,128)}, f32[1,5,128,1536]{3,2,1,0:T(8,128)}) fusion(f32[2,8,128,1536]{3,2,1,0:T(8,128)} %get-tuple-element.216, s32[]{:T(128)S(6)} %add.172, s32[]{:T(128)S(6)} %select_n.212), kind=kLoop, calls=%fused_computation.41.clone.1 | loop fusion | bytes 15728648 | tf_op jit(solution)/shard_map/while/body/eval_jaxpr/slice | solution.py:65
  244.1 8.7 %fusion.129 = f32[12,64,640]{2,1,0:T(8,128)S(1)} fusion(f32[640,12,128]{2,1,0:T(8,128)} %squeeze.24, f32[4,64,12,128]{3,1,2,0:T(8,128)} %get-tuple-element.219, s32[]{:T(128)S(6)} %select_n.213), kind=kOutput, calls=%fused_computation.5.clone.1 | convolution fusion | flops 754974720 | bytes 7602180 | tf_op jit(solution)/shard_map/while/body/eval_jaxpr/qhd,khd->hqk/dot_general | solution.py:27
  260.9 7.2 %fusion.133 = f32[4,64,12,128]{3,1,2,0:T(8,128)} fusion(f32[4,64,12,128]{3,1,2,0:T(8,128)} %get-tuple-element.202, s32[]{:T(128)} %get-tuple-element.201, f32[12,64,640]{2,1,0:T(8,128)S(1)} %copy-done.7, f32[640,12,128]{2,1,0:T(8,128)} %squeeze.25, f32[12,64]{1,0:T(8,128)S(1)} %get-tuple-element.188), kind=kOutput, calls=%fused_computation.13.clone.1 | convolution fusion | flops 755466240 | bytes 7605760 | tf_op jit(solution)/shard_map/while/body/eval_jaxpr/hqk,khd->qhd/dot_general | solution.py:33
  270.3 7.1 %constant_dynamic-slice_fusion.3 = (f32[1,5,128,1536]{3,2,1,0:T(8,128)}, f32[1,5,128,1536]{3,2,1,0:T(8,128)}) fusion(f32[2,8,128,1536]{3,2,1,0:T(8,128)} %get-tuple-element.216, s32[]{:T(128)S(6)} %add.172, s32[]{:T(128)S(6)} %select_n.212), kind=kLoop, calls=%fused_computation.41.clone.1 | loop fusion | bytes 15728648 | tf_op jit(solution)/shard_map/while/body/eval_jaxpr/slice | solution.py:65
  283.9 8.7 %fusion.129 = f32[12,64,640]{2,1,0:T(8,128)S(1)} fusion(f32[640,12,128]{2,1,0:T(8,128)} %squeeze.24, f32[4,64,12,128]{3,1,2,0:T(8,128)} %get-tuple-element.219, s32[]{:T(128)S(6)} %select_n.213), kind=kOutput, calls=%fused_computation.5.clone.1 | convolution fusion | flops 754974720 | bytes 7602180 | tf_op jit(solution)/shard_map/while/body/eval_jaxpr/qhd,khd->hqk/dot_general | solution.py:27
  300.7 7.2 %fusion.133 = f32[4,64,12,128]{3,1,2,0:T(8,128)} fusion(f32[4,64,12,128]{3,1,2,0:T(8,128)} %get-tuple-element.202, s32[]{:T(128)} %get-tuple-element.201, f32[12,64,640]{2,1,0:T(8,128)S(1)} %copy-done.7, f32[640,12,128]{2,1,0:T(8,128)} %squeeze.25, f32[12,64]{1,0:T(8,128)S(1)} %get-tuple-element.188), kind=kOutput, calls=%fused_computation.13.clone.1 | convolution fusion | flops 755466240 | bytes 7605760 | tf_op jit(solution)/shard_map/while/body/eval_jaxpr/hqk,khd->qhd/dot_general | solution.py:33
  310.2 7.1 %constant_dynamic-slice_fusion.3 = (f32[1,5,128,1536]{3,2,1,0:T(8,128)}, f32[1,5,128,1536]{3,2,1,0:T(8,128)}) fusion(f32[2,8,128,1536]{3,2,1,0:T(8,128)} %get-tuple-element.216, s32[]{:T(128)S(6)} %add.172, s32[]{:T(128)S(6)} %select_n.212), kind=kLoop, calls=%fused_computation.41.clone.1 | loop fusion | bytes 15728648 | tf_op jit(solution)/shard_map/while/body/eval_jaxpr/slice | solution.py:65
  323.7 8.7 %fusion.129 = f32[12,64,640]{2,1,0:T(8,128)S(1)} fusion(f32[640,12,128]{2,1,0:T(8,128)} %squeeze.24, f32[4,64,12,128]{3,1,2,0:T(8,128)} %get-tuple-element.219, s32[]{:T(128)S(6)} %select_n.213), kind=kOutput, calls=%fused_computation.5.clone.1 | convolution fusion | flops 754974720 | bytes 7602180 | tf_op jit(solution)/shard_map/while/body/eval_jaxpr/qhd,khd->hqk/dot_general | solution.py:27
  340.6 7.2 %fusion.133 = f32[4,64,12,128]{3,1,2,0:T(8,128)} fusion(f32[4,64,12,128]{3,1,2,0:T(8,128)} %get-tuple-element.202, s32[]{:T(128)} %get-tuple-element.201, f32[12,64,640]{2,1,0:T(8,128)S(1)} %copy-done.7, f32[640,12,128]{2,1,0:T(8,128)} %squeeze.25, f32[12,64]{1,0:T(8,128)S(1)} %get-tuple-element.188), kind=kOutput, calls=%fused_computation.13.clone.1 | convolution fusion | flops 755466240 | bytes 7605760 | tf_op jit(solution)/shard_map/while/body/eval_jaxpr/hqk,khd->qhd/dot_general | solution.py:33
  355.0 7.4 %all-to-all-start = ((f32[4,4,16,1536]{3,2,0,1:T(8,128)}), f32[4,4,16,1536]{3,2,0,1:T(8,128)S(1)}, u32[]{:S(2)}, u32[]{:S(2)}) async-start(f32[4,4,16,1536]{3,2,0,1:T(8,128)} %copy.33), calls=%async_computation | async-start | bytes 3145728 | tf_op jit(solution)/shard_map/all_to_all | solution.py:115
  363.3 36.4 %all-to-all-done = f32[4,4,16,1536]{3,2,0,1:T(8,128)S(1)} async-done(((f32[4,4,16,1536]{3,2,0,1:T(8,128)}), f32[4,4,16,1536]{3,2,0,1:T(8,128)S(1)}, u32[]{:S(2)}, u32[]{:S(2)}) %all-to-all-start) | async-done | bytes 1572896 | tf_op jit(solution)/shard_map/all_to_all | solution.py:115
  407.2 40.1 %all_to_all.33 = f32[16,1,16,1536]{3,2,1,0:T(8,128)S(1)} all-to-all(f32[16,1,16,1536]{3,2,1,0:T(8,128)} %bitcast.75), channel_id=1, replica_groups=mesh['grp'=2,'frm'=4,'head'=2,'pos'=2] {'frm'}, dimensions={0} | all-to-all | bytes 3145728 | tf_op jit(solution)/shard_map/all_to_all | solution.py:124
  (98 shorter events, 98.7 us)
Async XLA Ops:
  6.5 17.2 %all-gather.5.cloned.1.call-start = ((), (), s32[]{:S(2)}) async-start(), calls=%async_computation.2 | async-start | bytes 4718592 | tf_op jit(solution)/shard_map/all_gather | solution.py:51
  7.3 31.4 %all-gather.7.cloned.1.call-start = ((), (), s32[]{:S(2)}) async-start(), calls=%async_computation.3 | async-start | bytes 4718592 | tf_op jit(solution)/shard_map/all_gather | solution.py:52
  8.0 92.2 %all-gather.9.cloned.1.call-start = ((), (), s32[]{:S(2)}) async-start(), calls=%async_computation.4 | async-start | bytes 3538944 | tf_op jit(solution)/shard_map/all_gather | solution.py:79
  10.1 153.0 %all-gather.11.cloned.1.call-start = ((), (), s32[]{:S(2)}) async-start(), calls=%async_computation.5 | async-start | bytes 3538944 | tf_op jit(solution)/shard_map/all_gather | solution.py:80
  44.6 8.3 %copy-start.6 = (s32[12]{0:T(128)S(1)}, s32[12]{0:T(128)}, u32[]{:S(2)}) copy-start(s32[12]{0:T(128)} %param.12) | copy-start | bytes 148
  44.6 134.3 %collective-permute-start = (f32[2,2,128,1536]{3,2,1,0:T(8,128)}, f32[2,2,128,1536]{3,2,1,0:T(8,128)}, u32[]{:S(2)}, u32[]{:S(2)}) collective-permute-start(f32[2,2,128,1536]{3,2,1,0:T(8,128)} %get-tuple-element.134), channel_id=1, source_target_pairs={{0,4},{4,8},{8,12},{1,5},{5,9},{9,13},{2,6},{6,10},{10,14},{3,7},{... | collective-permute-start | bytes 9437192 | tf_op jit(solution)/shard_map/ppermute | solution.py:19
  50.0 128.9 %collective-permute-start.1 = (f32[2,2,128,1536]{3,2,1,0:T(8,128)}, f32[2,2,128,1536]{3,2,1,0:T(8,128)}, u32[]{:S(2)}, u32[]{:S(2)}) collective-permute-start(f32[2,2,128,1536]{3,2,1,0:T(8,128)} %get-tuple-element.135), channel_id=1, source_target_pairs={{4,0},{8,4},{12,8},{5,1},{9,5},{13,9},{6,2},{10,6},{14,10},{7,3},{... | collective-permute-start | bytes 9437192 | tf_op jit(solution)/shard_map/ppermute | solution.py:20
  108.0 2.6 copy-start
  176.2 2.7 copy-start.1
  178.9 9.6 %copy-start.4 = (s32[12]{0:T(128)S(1)}, s32[12]{0:T(128)}, u32[]{:S(2)}) copy-start(s32[12]{0:T(128)} %param.11) | copy-start | bytes 148
  215.5 5.5 %copy-start.7 = (f32[12,64,640]{2,1,0:T(8,128)S(1)}, f32[12,64,640]{2,1,0:T(8,128)}, u32[]{:S(2)}) copy-start(f32[12,64,640]{2,1,0:T(8,128)} %get-tuple-element.186) | copy-start | bytes 5898244 | tf_op jit(solution)/shard_map/while
  255.4 5.5 %copy-start.7 = (f32[12,64,640]{2,1,0:T(8,128)S(1)}, f32[12,64,640]{2,1,0:T(8,128)}, u32[]{:S(2)}) copy-start(f32[12,64,640]{2,1,0:T(8,128)} %get-tuple-element.186) | copy-start | bytes 5898244 | tf_op jit(solution)/shard_map/while
  295.2 5.5 %copy-start.7 = (f32[12,64,640]{2,1,0:T(8,128)S(1)}, f32[12,64,640]{2,1,0:T(8,128)}, u32[]{:S(2)}) copy-start(f32[12,64,640]{2,1,0:T(8,128)} %get-tuple-element.186) | copy-start | bytes 5898244 | tf_op jit(solution)/shard_map/while
  335.1 5.5 %copy-start.7 = (f32[12,64,640]{2,1,0:T(8,128)S(1)}, f32[12,64,640]{2,1,0:T(8,128)}, u32[]{:S(2)}) copy-start(f32[12,64,640]{2,1,0:T(8,128)} %get-tuple-element.186) | copy-start | bytes 5898244 | tf_op jit(solution)/shard_map/while
  355.0 7.7 %copy-start.5 = (s32[12]{0:T(128)S(1)}, s32[12]{0:T(128)}, u32[]{:S(2)}) copy-start(s32[12]{0:T(128)} %param.13) | copy-start | bytes 148
  355.0 44.8 %all-to-all-start = ((f32[4,4,16,1536]{3,2,0,1:T(8,128)}), f32[4,4,16,1536]{3,2,0,1:T(8,128)S(1)}, u32[]{:S(2)}, u32[]{:S(2)}) async-start(f32[4,4,16,1536]{3,2,0,1:T(8,128)} %copy.33), calls=%async_computation | async-start | bytes 3145728 | tf_op jit(solution)/shard_map/all_to_all | solution.py:115
  399.8 1.1 copy-start.3
  447.3 1.4 copy-start.2
Sparse Core Ops, SparseCore 0:
  8.9 14.8 all-gather.4
  25.3 13.2 all-gather.6
  40.2 59.9 all-gather.8
  101.7 61.3 all-gather.10
where the time goes:
time: 458 us; the launch traced here: 457 us
  waiting for transfers between devices  159 us (35%)
  local copies, waits for them, and re-layouts  102 us (22%)
  matrix products  85.3 us (19%)
  blocking collectives  40.1 us (9%)
  other arithmetic  29.7 us (6%)
  starting transfers between devices  14.3 us (3%)
  loops' own time  13.3 us (3%)
  between operations  13.3 us (3%)
    all_gather x1, waiting for transfers between devices, shards(): lax.all_gather(frame_values, ('frm', 'pos'), axis=0, tiled=True)  50.7 us
    all_gather x1, waiting for transfers between devices, shards(): key_part = lax.all_gather(frame_keys, ('frm', 'pos'), axis=0, tiled=True)  44 us
    all_to_all x1, blocking collectives, shards(): lax.all_to_all(filtered_block, 'frm', split_axis=0, concat_axis=1, tiled=...  40.1 us
    all_to_all x1, waiting for transfers between devices, shards(): lax.all_to_all(global_grid - local_grid, 'frm', split_axis=1, concat_axis...  36.4 us
    dot_general x4, matrix products, attend(): jnp.einsum('qhd,khd->hqk', query_rows, key_rows, precision=lax.Precision....  34.7 us
    dot_general x4, matrix products, attend(): jnp.einsum('hqk,khd->qhd', weights / row_total, value_rows, precision=lax...  29 us
    slice x4, local copies, waits for them, and re-layouts, local_frame(): near_values = block[1].reshape(span_rows, heads_local, DH)  28.4 us
    squeeze x4, local copies, waits for them, and re-layouts, local_frame(): near_values = block[1].reshape(span_rows, heads_local, DH)  22 us
  transfers between devices with their start and end apart: 7, of which 5 were waited for; matrix products, arithmetic and copies ran while one was open for 9% of the time, Pallas kernels for 0%

commit v1 on v0

v1 whole, which is shorter than its diff:
```python
import functools
import math

import jax
import jax.numpy as jnp
import numpy as np
from jax import lax
from jax.experimental import pallas as pl
from jax.experimental.pallas import tpu as pltpu
from jax.sharding import PartitionSpec as P

DH = 128
KSTRIDE = 4
MESH = pl.DeviceIdType.MESH
NEG = -1e30


def split_two(x):
    high = x.astype(jnp.bfloat16)
    low = (x - high.astype(jnp.float32)).astype(jnp.bfloat16)
    return high, low


def soft_rows(q_wide, keys, values, bias):
    rows = q_wide.shape[0]
    scores = lax.dot_general(
        q_wide, keys, (((1,), (1,)), ((), ())), preferred_element_type=jnp.float32
    )
    scores = scores + bias
    highest = jnp.max(scores, axis=1, keepdims=True)
    weights = jnp.exp(scores - highest)
    total = jnp.sum(weights, axis=1, keepdims=True)
    both = jnp.concatenate(split_two(weights), axis=0)
    wide = jnp.dot(both, values, preferred_element_type=jnp.float32)
    summed = (wide[:rows, :DH] + wide[:rows, DH:]) + (wide[rows:, :DH] + wide[rows:, DH:])
    return summed / total


def fill_split(key, value, keys_wide, values_wide, row, count):
    kh, kl = split_two(key)
    vh, vl = split_two(value)
    rows = pl.ds(row, count)
    keys_wide[rows, 0:DH] = kh
    keys_wide[rows, DH : 2 * DH] = kh
    keys_wide[rows, 2 * DH : 3 * DH] = kl
    keys_wide[rows, 3 * DH : 4 * DH] = kl
    values_wide[rows, 0:DH] = vh
    values_wide[rows, DH : 2 * DH] = vl


def kernel(
    sizes,
    win_ref, str_ref, cut_ref, basis_ref, q_ref, k_ref, v_ref, out_ref,
    ext, far, rowbuf, coef, rsum, lsum, ks, vs, kgs, vgs,
    x_own, x_send, x_recv, hr_send, hr_recv, hl_send, hl_recv, k_send, k_recv,
    cr_send, cr_recv, cl_send, cl_recv, o_own, o_send, o_recv,
):
    F, S, H, SHARED, Z, W, NC = sizes
    TOK = 2 * S
    z = lax.axis_index("frm")
    p = lax.axis_index("pos")
    other = 1 - p
    has_right = z < Z - 1
    has_left = z > 0
    right = jnp.minimum(z + 1, Z - 1)
    left = jnp.maximum(z - 1, 0)
    to_right, to_left, to_other = {"frm": right}, {"frm": left}, {"pos": other}

    def remote(src, dst, send, recv, to):
        return pltpu.make_async_remote_copy(
            src_ref=src, dst_ref=dst, send_sem=send, recv_sem=recv, device_id=to, device_id_type=MESH
        )

    def col(half, j):
        return pl.ds(pl.multiple_of((half * (H - SHARED) + j) * DH, DH), DH)

    my_rows = pl.ds(pl.multiple_of(p * S, S), S)
    other_rows = pl.ds(pl.multiple_of(other * S, S), S)

    def place(which, j, rows):
        if which == 0:
            return rowbuf.at[j, :, rows]
        return ext.at[j, which - 1, pl.ds(W, F), rows]

    sources = (q_ref, k_ref, v_ref)

    def own_copy(which, j):
        return pltpu.make_async_copy(
            sources[which].at[:, :, col(p, j)], place(which, j, my_rows), x_own.at[which, j]
        )

    def swap(which, j):
        return remote(
            sources[which].at[:, :, col(other, j)], place(which, j, my_rows),
            x_send.at[which, j], x_recv.at[which, j], to_other,
        )

    def halo_right(j):
        return remote(
            ext.at[j, :, pl.ds(F, W)], ext.at[j, :, pl.ds(0, W)], hr_send.at[j], hr_recv.at[j], to_right
        )

    def halo_left(j):
        return remote(
            ext.at[j, :, pl.ds(W, W)], ext.at[j, :, pl.ds(F + W, W)], hl_send.at[j], hl_recv.at[j], to_left
        )

    def key_copy(src, j, g, to):
        return remote(src, far.at[j, :, g], k_send.at[j, g], k_recv.at[j, g], to)

    def key_here(j, g, to):
        return key_copy(far.at[j, :, g], j, g, to)

    def sum_right(j):
        return remote(rsum.at[j], rsum.at[j], cr_send.at[j], cr_recv.at[j], to_right)

    def sum_left(j):
        return remote(lsum.at[j], lsum.at[j], cl_send.at[j], cl_recv.at[j], to_left)

    def out_own(j):
        return pltpu.make_async_copy(
            rowbuf.at[j, :, my_rows], out_ref.at[:, :, col(p, j)], o_own.at[j]
        )

    def out_other(j):
        return remote(
            rowbuf.at[j, :, other_rows], out_ref.at[:, :, col(p, j)], o_send.at[j], o_recv.at[j], to_other
        )

    barrier = pltpu.get_barrier_semaphore()
    pl.semaphore_signal(barrier, inc=1, device_id=to_other, device_id_type=MESH)

    @pl.when(has_right)
    def _():
        pl.semaphore_signal(barrier, inc=1, device_id=to_right, device_id_type=MESH)

    @pl.when(has_left)
    def _():
        pl.semaphore_signal(barrier, inc=1, device_id=to_left, device_id_type=MESH)

    pl.semaphore_wait(barrier, 1 + has_right.astype(jnp.int32) + has_left.astype(jnp.int32))

    def alone(half, j):
        if SHARED == 0:
            return j >= 0
        return jnp.where(half == 0, j < H - SHARED, j >= SHARED)

    order = (1, 2, 0)

    @pl.loop(0, H)
    def _(j):
        for which in order:
            swap(which, j).start()
            own_copy(which, j).start()

    def zero_halo(first):
        @pl.loop(0, H)
        def _(j):
            ext[j, :, first : first + W] = jnp.zeros((2, W, TOK, DH), jnp.float32)

    @pl.when(jnp.logical_not(has_left))
    def _():
        zero_halo(0)

    @pl.when(jnp.logical_not(has_right))
    def _():
        zero_halo(F + W)

    def arrive(which, j):
        own_copy(which, j).wait()
        swap(which, j).wait_recv()

    def compute(j):
        head = p * (H - SHARED) + j
        window = win_ref[head]
        stride = str_ref[head]
        cutoff = cut_ref[head]
        for e in range(F + 2 * W):
            fill_split(ext[j, 0, e], ext[j, 1, e], ks, vs, e * TOK, TOK)
        far[j, :, z] = ext[j, :, W]

        @pl.when(has_right)
        def _():
            far[j, :, z + 1] = ext[j, :, F + W]

        for g in range(Z):
            fill_split(far[j, 0, g], far[j, 1, g], kgs, vgs, g * TOK, TOK)

        def bias_row(flags):
            return jnp.concatenate(
                [jnp.full((1, TOK), jnp.where(ok, 0.0, NEG), jnp.float32) for ok in flags], axis=1
            )

        far_bias = bias_row([((g * KSTRIDE) & (stride - 1)) == 0 for g in range(Z)])
        diffs = []
        for i in range(F):
            qh, ql = split_two(rowbuf[j, i] * (DH**-0.5))
            q_wide = jnp.concatenate([qh, ql, qh, ql], axis=1)
            flags = []
            for off in range(-W, W + 1):
                frame = z * F + i + off
                flags.append((abs(off) <= window) & (frame >= 0) & (frame < Z * F))
            near_rows = pl.ds(i * TOK, (2 * W + 1) * TOK)
            local = soft_rows(q_wide, ks[near_rows], vs[near_rows], bias_row(flags))
            wide = soft_rows(q_wide, kgs[...], vgs[...], far_bias)
            rowbuf[j, i] = local
            diffs.append(wide - local)
        for c in range(NC):
            acc = diffs[0] * basis_ref[(z * F) * NC + c]
            for i in range(1, F):
                acc = acc + diffs[i] * basis_ref[(z * F + i) * NC + c]
            keep = jnp.where((c + 1) // 2 <= cutoff, 1.0, 0.0)
            coef[j, c] = acc * keep

    def finish(j):
        totals = [(rsum[j, c] - coef[j, c]) + lsum[j, c] for c in range(NC)]
        for i in range(F):
            acc = rowbuf[j, i]
            for c in range(NC):
                acc = acc + totals[c] * basis_ref[(z * F + i) * NC + c]
            rowbuf[j, i] = acc
        out_own(j).start()

        @pl.when(alone(p, j))
        def _():
            out_other(j).start()

    reach = Z - 1
    last = jnp.maximum(z, Z - 1 - z)

    def valid(j):
        return (j >= 0) & (j < H)

    @pl.loop(0, H + 2 * reach)
    def _(t):
        @pl.when(t < H)
        def _():
            arrive(1, t)
            arrive(2, t)

            @pl.when(has_right)
            def _():
                key_copy(ext.at[t, :, W], t, z, to_right).start()
                halo_right(t).start()

            @pl.when(has_left)
            def _():
                halo_left(t).start()

        @pl.when(valid(t - 1) & has_right)
        def _():
            halo_left(t - 1).wait_recv()

            @pl.when(has_left)
            def _():
                key_copy(ext.at[t - 1, :, F + W], t - 1, z + 1, to_left).start()

        for d in range(1, Z):
            @pl.when(valid(t - d) & (z - d >= 0))
            def _():
                key_here(t - d, z - d, to_right).wait_recv()

                @pl.when(has_right)
                def _():
                    key_here(t - d, z - d, to_right).start()

        for d in range(2, Z):
            @pl.when(valid(t - d) & (z + d < Z))
            def _():
                key_here(t - d, z + d, to_left).wait_recv()

                @pl.when(has_left)
                def _():
                    key_here(t - d, z + d, to_left).start()

        now = t - reach

        @pl.when(valid(now))
        def _():
            arrive(0, now)

            @pl.when(has_left)
            def _():
                halo_right(now).wait_recv()

            compute(now)

        jr = now - z

        @pl.when(valid(jr))
        def _():
            @pl.when(has_left)
            def _():
                sum_right(jr).wait_recv()
                rsum[jr] = rsum[jr] + coef[jr]

            @pl.when(jnp.logical_not(has_left))
            def _():
                rsum[jr] = coef[jr]

            @pl.when(has_right)
            def _():
                sum_right(jr).start()

        jl = now - (Z - 1 - z)

        @pl.when(valid(jl))
        def _():
            @pl.when(has_right)
            def _():
                sum_left(jl).wait_recv()
                lsum[jl] = lsum[jl] + coef[jl]

            @pl.when(jnp.logical_not(has_right))
            def _():
                lsum[jl] = coef[jl]

            @pl.when(has_left)
            def _():
                sum_left(jl).start()

        jf = now - last

        @pl.when(valid(jf))
        def _():
            finish(jf)

    @pl.loop(0, H)
    def _(j):
        for which in range(3):
            swap(which, j).wait_send()

        @pl.when(has_right)
        def _():
            halo_right(j).wait_send()
            sum_right(j).wait_send()
            key_copy(ext.at[j, :, W], j, z, to_right).wait_send()

        @pl.when(has_left)
        def _():
            halo_left(j).wait_send()
            sum_left(j).wait_send()

        @pl.when(has_left & has_right)
        def _():
            key_copy(ext.at[j, :, F + W], j, z + 1, to_left).wait_send()

        for d in range(1, Z):
            @pl.when((z - d >= 0) & has_right)
            def _():
                key_here(j, z - d, to_right).wait_send()

        for d in range(2, Z):
            @pl.when((z + d < Z) & has_left)
            def _():
                key_here(j, z + d, to_left).wait_send()

        out_own(j).wait()

        @pl.when(alone(p, j))
        def _():
            out_other(j).wait_send()

        @pl.when(alone(other, j))
        def _():
            out_other(j).wait_recv()


def basis_table(total_frames, top):
    frames = np.arange(total_frames)
    columns = [np.full(total_frames, math.sqrt(1.0 / total_frames))]
    for k in range(1, top + 1):
        phase = 2.0 * math.pi * ((k * frames) % total_frames) / total_frames
        columns.append(math.sqrt(2.0 / total_frames) * np.cos(phase))
        columns.append(math.sqrt(2.0 / total_frames) * np.sin(phase))
    return np.stack(columns, axis=1).astype(np.float32)


def shards(queries, key_states, value_states, windows, strides, cutoffs):
    F, S, channels = queries.shape
    Z = lax.axis_size("frm")
    heads = channels // DH
    H = (heads + 1) // 2
    SHARED = 2 * H - heads
    W = F // 2
    assert lax.axis_size("pos") == 2 and F == KSTRIDE
    basis = basis_table(F * Z, F * Z // 8)
    NC = basis.shape[1]
    TOK = 2 * S
    dma = pltpu.SemaphoreType.DMA
    f32, bf16 = jnp.float32, jnp.bfloat16
    return pl.pallas_call(
        functools.partial(kernel, (F, S, H, SHARED, Z, W, NC)),
        out_shape=jax.ShapeDtypeStruct(queries.shape, f32),
        in_specs=[pl.BlockSpec(memory_space=pltpu.SMEM)] * 4 + [pl.BlockSpec(memory_space=pl.ANY)] * 3,
        out_specs=pl.BlockSpec(memory_space=pl.ANY),
        scratch_shapes=[
            pltpu.VMEM((H, 2, F + 2 * W, TOK, DH), f32),
            pltpu.VMEM((H, 2, Z, TOK, DH), f32),
            pltpu.VMEM((H, F, TOK, DH), f32),
            pltpu.VMEM((H, NC, TOK, DH), f32),
            pltpu.VMEM((H, NC, TOK, DH), f32),
            pltpu.VMEM((H, NC, TOK, DH), f32),
            pltpu.VMEM(((F + 2 * W) * TOK, 4 * DH), bf16),
            pltpu.VMEM(((F + 2 * W) * TOK, 2 * DH), bf16),
            pltpu.VMEM((Z * TOK, 4 * DH), bf16),
            pltpu.VMEM((Z * TOK, 2 * DH), bf16),
            dma((3, H)), dma((3, H)), dma((3, H)),
            dma((H,)), dma((H,)), dma((H,)), dma((H,)),
            dma((H, Z)), dma((H, Z)),
            dma((H,)), dma((H,)), dma((H,)), dma((H,)),
            dma((H,)), dma((H,)), dma((H,)),
        ],
        compiler_params=pltpu.CompilerParams(
            collective_id=0, has_side_effects=True, vmem_limit_bytes=60 * 1024 * 1024
        ),
    )(windows, strides, cutoffs, jnp.asarray(basis.reshape(-1)), queries, key_states, value_states)


def solution(mesh):
    in_specs = (
        P(("grp", "frm"), "pos", "head"),
        P(("grp", "frm"), "pos", "head"),
        P(("grp", "frm"), "pos", "head"),
        P("head"),
        P("head"),
        P("head"),
    )
    out_specs = P(("grp", "frm"), "pos", "head")
    return jax.shard_map(shards, mesh=mesh, in_specs=in_specs, out_specs=out_specs, check_vma=False)
```

time: 458 us -> 145 us (0.32)
  waiting for transfers between devices: 159 us -> 0 us
  Pallas kernels: 0 us -> 143 us
  local copies, waits for them, and re-layouts: 102 us -> 2.66 us
  matrix products: 85.3 us -> 0 us
  blocking collectives: 40.1 us -> 0 us
  other arithmetic: 29.7 us -> 0 us
  starting transfers between devices: 14.3 us -> 0 us
  loops' own time: 13.3 us -> 0 us
  between operations: 13.3 us -> 0.01 us
    pallas_call x0 -> x1, Pallas kernels: none -> 143 us  [shards(): pl.pallas_call(functools.partial(kernel, (F, S, H, SHARED, Z, W, NC)), ou...]
    all_gather x4 -> x0, waiting for transfers between devices: 121 us -> none  [the longest x1 50.7 us: shards(): lax.all_gather(frame_values, ('frm', 'pos'), axis=0, tiled=True)]
    dot_general x13 -> x0, matrix products: 85.3 us -> none  [the longest x4 34.7 us: attend(): jnp.einsum('qhd,khd->hqk', query_rows, key_rows, precision=lax.Precision....]
    squeeze x8 -> x0, local copies, waits for them, and re-layouts: 43.5 us -> none  [the longest x4 22 us: local_frame(): near_values = block[1].reshape(span_rows, heads_local, DH)]
    all_to_all x1 -> x0, blocking collectives: 40.1 us -> none  [shards(): lax.all_to_all(filtered_block, 'frm', split_axis=0, concat_axis=1, tiled=...]
    all_to_all x1 -> x0, waiting for transfers between devices: 36.4 us -> none  [shards(): lax.all_to_all(global_grid - local_grid, 'frm', split_axis=1, concat_axis...]
    slice x6 -> x0, local copies, waits for them, and re-layouts: 30.4 us -> none  [the longest x4 28.4 us: local_frame(): near_values = block[1].reshape(span_rows, heads_local, DH)]
    another operation x1 -> x0, loops' own time: 13.3 us -> none  [shards(): lax.map(local_frame, jnp.arange(frames_dev, dtype=jnp.int32))]
  transfers between devices with their start and end apart: 7 -> 0, of which waited for: 5 -> 0; matrix products, arithmetic and copies ran while one was open for 9% -> 0% of each run, Pallas kernels for 0% -> 0%
where the time goes in v1:
time: 145 us
  Pallas kernels  143 us (99%)
  local copies, waits for them, and re-layouts  2.66 us (2%)
    pallas_call x1, Pallas kernels, shards(): pl.pallas_call(functools.partial(kernel, (F, S, H, SHARED, Z, W, NC)), ou...  143 us

profile of v1, /device:TPU:0, one launch (start us, length us, event | category | flops | bytes accessed | tf_op | source)
XLA Modules:
  0.0 145.3 jit_solution(1680877163119227600)
XLA Ops:
  0.0 142.6 %shard_map.73 = f32[4,64,1536]{2,1,0:T(8,128)} custom-call(s32[12]{0:T(128)} %win_ref.1, s32[12]{0:T(128)} %str_ref.1, s32[12]{0:T(128)} %cut_ref.1, f32[80]{0:T(128)} %constant.2.clone.basis_ref, f32[4,64,1536]{2,1,0:T(8,128)} %q_ref.1, f32[4,64,1536]{2,1,0:T(8,128)} %k_ref.1, f32[4,64,1536]{2,1,0:T(8,128)} %v_ref.1), custom_call_target="tpu_custom_call" | custom-call | tf_op jit(solution)/shard_map/pallas_call | solution.py:392
  142.6 2.7 %copy.9 = f32[4,64,1536]{2,1,0:T(8,128)} copy(f32[4,64,1536]{2,1,0:T(8,128)} %shard_map.73) | data formatting | bytes 3145728

commit v2 on v1

--- a/solution.py
+++ b/solution.py
@@ -51,9 +51,9 @@
 def kernel(
     sizes,
     win_ref, str_ref, cut_ref, basis_ref, q_ref, k_ref, v_ref, out_ref,
-    ext, far, rowbuf, coef, rsum, lsum, ks, vs, kgs, vgs,
+    ext, far, rowbuf, coef, rsum, lsum, edge_r, edge_l, dbuf, ks, vs, kgs, vgs,
     x_own, x_send, x_recv, hr_send, hr_recv, hl_send, hl_recv, k_send, k_recv,
-    cr_send, cr_recv, cl_send, cl_recv, o_own, o_send, o_recv,
+    cr_send, cr_recv, cl_send, cl_recv, q_send, q_recv, o_own, o_send, o_recv,
 ):
     F, S, H, SHARED, Z, W, NC = sizes
     TOK = 2 * S
@@ -64,6 +64,10 @@
     has_left = z > 0
     right = jnp.minimum(z + 1, Z - 1)
     left = jnp.maximum(z - 1, 0)
+    is_first = z == 0
+    is_last = z == Z - 1
+    is_helper = z == Z - 2
+    keys_right = z < Z - 2
     to_right, to_left, to_other = {"frm": right}, {"frm": left}, {"pos": other}
 
     def remote(src, dst, send, recv, to):
@@ -79,7 +83,7 @@
 
     def place(which, j, rows):
         if which == 0:
-            return rowbuf.at[j, :, rows]
+            return rowbuf.at[j, pl.ds(0, F), rows]
         return ext.at[j, which - 1, pl.ds(W, F), rows]
 
     sources = (q_ref, k_ref, v_ref)
@@ -111,20 +115,39 @@
     def key_here(j, g, to):
         return key_copy(far.at[j, :, g], j, g, to)
 
-    def sum_right(j):
+    def sum_right_full(j):
         return remote(rsum.at[j], rsum.at[j], cr_send.at[j], cr_recv.at[j], to_right)
 
-    def sum_left(j):
+    def sum_right_first(j):
+        part = rsum.at[j, pl.ds(0, F)]
+        return remote(part, part, cr_send.at[j], cr_recv.at[j], to_right)
+
+    def sum_right_last(j):
+        return remote(edge_r.at[j], rsum.at[j, pl.ds(0, F)], cr_send.at[j], cr_recv.at[j], to_right)
+
+    def sum_left_full(j):
         return remote(lsum.at[j], lsum.at[j], cl_send.at[j], cl_recv.at[j], to_left)
+
+    def sum_left_first(j):
+        part = lsum.at[j, pl.ds(0, F)]
+        return remote(part, part, cl_send.at[j], cl_recv.at[j], to_left)
+
+    def sum_left_last(j):
+        return remote(edge_l.at[j], lsum.at[j, pl.ds(0, F)], cl_send.at[j], cl_recv.at[j], to_left)
+
+    def query_left(j):
+        return remote(
+            rowbuf.at[j, pl.ds(0, F)], rowbuf.at[j, pl.ds(F, F)], q_send.at[j], q_recv.at[j], to_left
+        )
 
     def out_own(j):
         return pltpu.make_async_copy(
-            rowbuf.at[j, :, my_rows], out_ref.at[:, :, col(p, j)], o_own.at[j]
+            rowbuf.at[j, pl.ds(0, F), my_rows], out_ref.at[:, :, col(p, j)], o_own.at[j]
         )
 
     def out_other(j):
         return remote(
-            rowbuf.at[j, :, other_rows], out_ref.at[:, :, col(p, j)], o_send.at[j], o_recv.at[j], to_other
+            rowbuf.at[j, pl.ds(0, F), other_rows], out_ref.at[:, :, col(p, j)], o_send.at[j], o_recv.at[j], to_other
         )
 
     barrier = pltpu.get_barrier_semaphore()
@@ -174,79 +197,149 @@
         head = p * (H - SHARED) + j
         window = win_ref[head]
         stride = str_ref[head]
-        cutoff = cut_ref[head]
         for e in range(F + 2 * W):
             fill_split(ext[j, 0, e], ext[j, 1, e], ks, vs, e * TOK, TOK)
-        far[j, :, z] = ext[j, :, W]
-
-        @pl.when(has_right)
-        def _():
-            far[j, :, z + 1] = ext[j, :, F + W]
-
-        for g in range(Z):
-            fill_split(far[j, 0, g], far[j, 1, g], kgs, vgs, g * TOK, TOK)
 
         def bias_row(flags):
             return jnp.concatenate(
                 [jnp.full((1, TOK), jnp.where(ok, 0.0, NEG), jnp.float32) for ok in flags], axis=1
             )
 
-        far_bias = bias_row([((g * KSTRIDE) & (stride - 1)) == 0 for g in range(Z)])
-        diffs = []
+        def wide_query(i):
+            qh, ql = split_two(rowbuf[j, i] * (DH**-0.5))
+            return jnp.concatenate([qh, ql, qh, ql], axis=1)
+
+        @pl.when(jnp.logical_not(is_last))
+        def _():
+            far[j, :, z] = ext[j, :, W]
+            far[j, :, z + 1] = ext[j, :, F + W]
+            for g in range(Z):
+                fill_split(far[j, 0, g], far[j, 1, g], kgs, vgs, g * TOK, TOK)
+            far_bias = bias_row([((g * KSTRIDE) & (stride - 1)) == 0 for g in range(Z)])
+
+            @pl.loop(0, jnp.where(is_helper, 2 * F, F))
+            def _(i):
+                dbuf[i] = soft_rows(wide_query(i), kgs[...], vgs[...], far_bias)
+
+        @pl.when(is_last)
+        def _():
+            dbuf[0:F] = jnp.zeros((F, TOK, DH), jnp.float32)
+
         for i in range(F):
-            qh, ql = split_two(rowbuf[j, i] * (DH**-0.5))
-            q_wide = jnp.concatenate([qh, ql, qh, ql], axis=1)
             flags = []
             for off in range(-W, W + 1):
                 frame = z * F + i + off
                 flags.append((abs(off) <= window) & (frame >= 0) & (frame < Z * F))
             near_rows = pl.ds(i * TOK, (2 * W + 1) * TOK)
-            local = soft_rows(q_wide, ks[near_rows], vs[near_rows], bias_row(flags))
-            wide = soft_rows(q_wide, kgs[...], vgs[...], far_bias)
+            local = soft_rows(wide_query(i), ks[near_rows], vs[near_rows], bias_row(flags))
             rowbuf[j, i] = local
-            diffs.append(wide - local)
+            dbuf[i] = dbuf[i] - local
         for c in range(NC):
-            acc = diffs[0] * basis_ref[(z * F) * NC + c]
-            for i in range(1, F):
-                acc = acc + diffs[i] * basis_ref[(z * F + i) * NC + c]
-            keep = jnp.where((c + 1) // 2 <= cutoff, 1.0, 0.0)
-            coef[j, c] = acc * keep
+            coef[j, c] = keep_of(j, c) * project([dbuf[i] for i in range(F)], z, c)
+
+        @pl.when(is_helper)
+        def _():
+            for c in range(NC):
+                more = project([dbuf[F + i] for i in range(F)], Z - 1, c)
+                coef[j, c] = coef[j, c] + keep_of(j, c) * more
+
+        @pl.when(is_first)
+        def _():
+            rsum[j, 0:F] = dbuf[0:F]
+
+        @pl.when(is_last)
+        def _():
+            lsum[j, 0:F] = dbuf[0:F]
+
+    def keep_of(j, c):
+        return jnp.where((c + 1) // 2 <= cut_ref[p * (H - SHARED) + j], 1.0, 0.0)
+
+    def project(frames, at, c):
+        acc = frames[0] * basis_ref[at * F * NC + c]
+        for i in range(1, F):
+            acc = acc + frames[i] * basis_ref[(at * F + i) * NC + c]
+        return acc
+
+    def expand(start, totals, at, i):
+        for c in range(NC):
+            part = totals[c] * basis_ref[(at * F + i) * NC + c]
+            start = part if start is None else start + part
+        return start
 
     def finish(j):
-        totals = [(rsum[j, c] - coef[j, c]) + lsum[j, c] for c in range(NC)]
+        def ends(received):
+            totals = [coef[j, c] for c in range(NC)]
+            for i in range(F):
+                rowbuf[j, i] = expand(rowbuf[j, i] + received[j, i], totals, z, i)
+
+        @pl.when(is_first)
+        def _():
+            ends(lsum)
+
+        @pl.when(is_last)
+        def _():
+            ends(rsum)
+
+        @pl.when(has_left & has_right)
+        def _():
+            totals = [(rsum[j, c] - coef[j, c]) + lsum[j, c] for c in range(NC)]
+            for i in range(F):
+                rowbuf[j, i] = expand(rowbuf[j, i], totals, z, i)
+
+        out_own(j).start()
+
+        @pl.when(alone(p, j))
+        def _():
+            out_other(j).start()
+
+    def add_raw(sums, j, at):
+        raw = [sums[j, i] for i in range(F)]
+        for c in range(NC):
+            sums[j, c] = coef[j, c] + keep_of(j, c) * project(raw, at, c)
+
+    def fill_edge(edge, sums, j, at):
+        totals = [sums[j, c] for c in range(NC)]
         for i in range(F):
-            acc = rowbuf[j, i]
-            for c in range(NC):
-                acc = acc + totals[c] * basis_ref[(z * F + i) * NC + c]
-            rowbuf[j, i] = acc
-        out_own(j).start()
-
-        @pl.when(alone(p, j))
-        def _():
-            out_other(j).start()
-
-    reach = Z - 1
-    last = jnp.maximum(z, Z - 1 - z)
+            edge[j, i] = expand(None, totals, at, i)
+
+    delay = jnp.where(is_last, 1, jnp.maximum(z, Z - 1 - z))
+    right_delay = Z - 1 + z
+    left_delay = jnp.where(is_last, 1, 2 * Z - 4 - z)
+    last_delay = jnp.maximum(right_delay, left_delay)
+    from_first = z == 1
+    middle_in_right = (z > 1) & (z < Z - 1)
+    middle_in_left = (z > 0) & (z < Z - 2)
+    middle_out_right = (z > 0) & (z < Z - 2)
+    middle_out_left = (z > 1) & (z < Z - 1)
 
     def valid(j):
         return (j >= 0) & (j < H)
 
-    @pl.loop(0, H + 2 * reach)
+    @pl.loop(0, H + 2 * Z - 2)
     def _(t):
         @pl.when(t < H)
         def _():
             arrive(1, t)
             arrive(2, t)
 
+            @pl.when(keys_right)
+            def _():
+                key_copy(ext.at[t, :, W], t, z, to_right).start()
+
             @pl.when(has_right)
             def _():
-                key_copy(ext.at[t, :, W], t, z, to_right).start()
                 halo_right(t).start()
 
             @pl.when(has_left)
             def _():
                 halo_left(t).start()
 
+            arrive(0, t)
+
+            @pl.when(is_last)
+            def _():
+                query_left(t).start()
+
         @pl.when(valid(t - 1) & has_right)
         def _():
             halo_left(t - 1).wait_recv()
@@ -255,12 +348,12 @@
             def _():
                 key_copy(ext.at[t - 1, :, F + W], t - 1, z + 1, to_left).start()
 
-        for d in range(1, Z):
-            @pl.when(valid(t - d) & (z - d >= 0))
+        for d in range(1, Z - 1):
+            @pl.when(valid(t - d) & (z - d >= 0) & jnp.logical_not(is_last))
             def _():
                 key_here(t - d, z - d, to_right).wait_recv()
 
-                @pl.when(has_right)
+                @pl.when(keys_right)
                 def _():
                     key_here(t - d, z - d, to_right).start()
 
@@ -273,53 +366,87 @@
                 def _():
                     key_here(t - d, z + d, to_left).start()
 
-        now = t - reach
+        now = t - delay
 
         @pl.when(valid(now))
         def _():
-            arrive(0, now)
-
             @pl.when(has_left)
             def _():
                 halo_right(now).wait_recv()
 
+            @pl.when(is_helper)
+            def _():
+                query_left(now).wait_recv()
+
+            @pl.when(is_last)
+            def _():
+                query_left(now).wait_send()
+
             compute(now)
 
-        jr = now - z
+        jr = t - right_delay
 
         @pl.when(valid(jr))
         def _():
-            @pl.when(has_left)
-            def _():
-                sum_right(jr).wait_recv()
+            @pl.when(is_first)
+            def _():
+                sum_right_first(jr).start()
+
+            @pl.when(from_first)
+            def _():
+                sum_right_first(jr).wait_recv()
+                add_raw(rsum, jr, 0)
+
+            @pl.when(middle_in_right)
+            def _():
+                sum_right_full(jr).wait_recv()
                 rsum[jr] = rsum[jr] + coef[jr]
 
-            @pl.when(jnp.logical_not(has_left))
-            def _():
-                rsum[jr] = coef[jr]
-
-            @pl.when(has_right)
-            def _():
-                sum_right(jr).start()
-
-        jl = now - (Z - 1 - z)
+            @pl.when(is_last)
+            def _():
+                sum_right_last(jr).wait_recv()
+
+            @pl.when(middle_out_right)
+            def _():
+                sum_right_full(jr).start()
+
+            @pl.when(is_helper)
+            def _():
+                fill_edge(edge_r, rsum, jr, Z - 1)
+                sum_right_last(jr).start()
+
+        jl = t - left_delay
 
         @pl.when(valid(jl))
         def _():
-            @pl.when(has_right)
-            def _():
-                sum_left(jl).wait_recv()
+            @pl.when(is_last)
+            def _():
+                sum_left_first(jl).start()
+
+            @pl.when(is_helper)
+            def _():
+                sum_left_first(jl).wait_recv()
+                add_raw(lsum, jl, Z - 1)
+
+            @pl.when(middle_in_left)
+            def _():
+                sum_left_full(jl).wait_recv()
                 lsum[jl] = lsum[jl] + coef[jl]
 
-            @pl.when(jnp.logical_not(has_right))
-            def _():
-                lsum[jl] = coef[jl]
-
-            @pl.when(has_left)
-            def _():
-                sum_left(jl).start()
-
-        jf = now - last
+            @pl.when(is_first)
+            def _():
+                sum_left_last(jl).wait_recv()
+
+            @pl.when(middle_out_left)
+            def _():
+                sum_left_full(jl).start()
+
+            @pl.when(from_first)
+            def _():
+                fill_edge(edge_l, lsum, jl, 0)
+                sum_left_last(jl).start()
+
+        jf = t - last_delay
 
         @pl.when(valid(jf))
         def _():
@@ -330,23 +457,48 @@
         for which in range(3):
             swap(which, j).wait_send()
 
+        @pl.when(keys_right)
+        def _():
+            key_copy(ext.at[j, :, W], j, z, to_right).wait_send()
+
         @pl.when(has_right)
         def _():
             halo_right(j).wait_send()
-            sum_right(j).wait_send()
-            key_copy(ext.at[j, :, W], j, z, to_right).wait_send()
 
         @pl.when(has_left)
         def _():
             halo_left(j).wait_send()
-            sum_left(j).wait_send()
+
+        @pl.when(is_first)
+        def _():
+            sum_right_first(j).wait_send()
+
+        @pl.when(middle_out_right)
+        def _():
+            sum_right_full(j).wait_send()
+
+        @pl.when(is_helper)
+        def _():
+            sum_right_last(j).wait_send()
+
+        @pl.when(is_last)
+        def _():
+            sum_left_first(j).wait_send()
+
+        @pl.when(middle_out_left)
+        def _():
+            sum_left_full(j).wait_send()
+
+        @pl.when(from_first)
+        def _():
+            sum_left_last(j).wait_send()
 
         @pl.when(has_left & has_right)
         def _():
             key_copy(ext.at[j, :, F + W], j, z + 1, to_left).wait_send()
 
-        for d in range(1, Z):
-            @pl.when((z - d >= 0) & has_right)
+        for d in range(1, Z - 1):
+            @pl.when((z - d >= 0) & keys_right)
             def _():
                 key_here(j, z - d, to_right).wait_send()
 
@@ -383,9 +535,9 @@
     H = (heads + 1) // 2
     SHARED = 2 * H - heads
     W = F // 2
-    assert lax.axis_size("pos") == 2 and F == KSTRIDE
     basis = basis_table(F * Z, F * Z // 8)
     NC = basis.shape[1]
+    assert lax.axis_size("pos") == 2 and F == KSTRIDE and Z >= 3 and NC >= F
     TOK = 2 * S
     dma = pltpu.SemaphoreType.DMA
     f32, bf16 = jnp.float32, jnp.bfloat16
@@ -397,10 +549,13 @@
         scratch_shapes=[
             pltpu.VMEM((H, 2, F + 2 * W, TOK, DH), f32),
             pltpu.VMEM((H, 2, Z, TOK, DH), f32),
-            pltpu.VMEM((H, F, TOK, DH), f32),
+            pltpu.VMEM((H, 2 * F, TOK, DH), f32),
             pltpu.VMEM((H, NC, TOK, DH), f32),
             pltpu.VMEM((H, NC, TOK, DH), f32),
             pltpu.VMEM((H, NC, TOK, DH), f32),
+            pltpu.VMEM((H, F, TOK, DH), f32),
+            pltpu.VMEM((H, F, TOK, DH), f32),
+            pltpu.VMEM((2 * F, TOK, DH), f32),
             pltpu.VMEM(((F + 2 * W) * TOK, 4 * DH), bf16),
             pltpu.VMEM(((F + 2 * W) * TOK, 2 * DH), bf16),
             pltpu.VMEM((Z * TOK, 4 * DH), bf16),
@@ -409,7 +564,7 @@
             dma((H,)), dma((H,)), dma((H,)), dma((H,)),
             dma((H, Z)), dma((H, Z)),
             dma((H,)), dma((H,)), dma((H,)), dma((H,)),
-            dma((H,)), dma((H,)), dma((H,)),
+            dma((H,)), dma((H,)), dma((H,)), dma((H,)), dma((H,)),
         ],
         compiler_params=pltpu.CompilerParams(
             collective_id=0, has_side_effects=True, vmem_limit_bytes=60 * 1024 * 1024

time: 145 us -> 139 us (0.959)
  the two profiles are of different devices: /device:TPU:0 before, /device:TPU:27 now
where the time goes in v2:
time: 139 us
  Pallas kernels  137 us (99%)
  local copies, waits for them, and re-layouts  2.66 us (2%)
    pallas_call x1, Pallas kernels, shards(): pl.pallas_call(functools.partial(kernel, (F, S, H, SHARED, Z, W, NC)), ou...  137 us

profile of v2, /device:TPU:27, one launch (start us, length us, event | category | flops | bytes accessed | tf_op | source)
XLA Modules:
  0.0 139.2 jit_solution(10853931885254917367)
XLA Ops:
  0.0 136.6 %shard_map.73 = f32[4,64,1536]{2,1,0:T(8,128)} custom-call(s32[12]{0:T(128)} %win_ref.1, s32[12]{0:T(128)} %str_ref.1, s32[12]{0:T(128)} %cut_ref.1, f32[80]{0:T(128)} %constant.2.clone.basis_ref, f32[4,64,1536]{2,1,0:T(8,128)} %q_ref.1, f32[4,64,1536]{2,1,0:T(8,128)} %k_ref.1, f32[4,64,1536]{2,1,0:T(8,128)} %v_ref.1), custom_call_target="tpu_custom_call" | custom-call | tf_op jit(solution)/shard_map/pallas_call | solution.py:544
  136.6 2.7 %copy.9 = f32[4,64,1536]{2,1,0:T(8,128)} copy(f32[4,64,1536]{2,1,0:T(8,128)} %shard_map.73) | data formatting | bytes 3145728

commit v3 on v2

--- a/solution.py
+++ b/solution.py
@@ -168,13 +168,14 @@
             return j >= 0
         return jnp.where(half == 0, j < H - SHARED, j >= SHARED)
 
-    order = (1, 2, 0)
-
-    @pl.loop(0, H)
-    def _(j):
-        for which in order:
-            swap(which, j).start()
-            own_copy(which, j).start()
+    def fetch(which, j):
+        swap(which, j).start()
+        own_copy(which, j).start()
+
+    ahead = min(2, H)
+    for first in range(ahead):
+        fetch(1, first)
+        fetch(2, first)
 
     def zero_halo(first):
         @pl.loop(0, H)
@@ -302,10 +303,6 @@
         for i in range(F):
             edge[j, i] = expand(None, totals, at, i)
 
-    delay = jnp.where(is_last, 1, jnp.maximum(z, Z - 1 - z))
-    right_delay = Z - 1 + z
-    left_delay = jnp.where(is_last, 1, 2 * Z - 4 - z)
-    last_delay = jnp.maximum(right_delay, left_delay)
     from_first = z == 1
     middle_in_right = (z > 1) & (z < Z - 1)
     middle_in_left = (z > 0) & (z < Z - 2)
@@ -315,68 +312,85 @@
     def valid(j):
         return (j >= 0) & (j < H)
 
-    @pl.loop(0, H + 2 * Z - 2)
+    @pl.loop(0, H)
     def _(t):
-        @pl.when(t < H)
-        def _():
-            arrive(1, t)
-            arrive(2, t)
-
-            @pl.when(keys_right)
-            def _():
-                key_copy(ext.at[t, :, W], t, z, to_right).start()
-
-            @pl.when(has_right)
-            def _():
-                halo_right(t).start()
-
+        arrive(1, t)
+        arrive(2, t)
+
+        @pl.when(t + ahead < H)
+        def _():
+            fetch(1, t + ahead)
+            fetch(2, t + ahead)
+
+        @pl.when(keys_right)
+        def _():
+            key_copy(ext.at[t, :, W], t, z, to_right).start()
+
+        @pl.when(has_left)
+        def _():
+            halo_left(t).start()
+
+        @pl.when(has_right)
+        def _():
+            halo_right(t).start()
+
+    @pl.loop(0, H)
+    def _(t):
+        fetch(0, t)
+
+    @pl.loop(0, H)
+    def _(t):
+        arrive(0, t)
+
+        @pl.when(is_last)
+        def _():
+            query_left(t).start()
+
+    @pl.loop(0, H + Z - 2)
+    def _(t):
+        @pl.when(valid(t) & has_right & has_left)
+        def _():
+            halo_left(t).wait_recv()
+            key_copy(ext.at[t, :, F + W], t, z + 1, to_left).start()
+
+        for d in range(1, Z - 1):
+            @pl.when(valid(t - d + 1) & (z - d >= 0) & keys_right)
+            def _():
+                key_here(t - d + 1, z - d, to_right).wait_recv()
+                key_here(t - d + 1, z - d, to_right).start()
+
+        for d in range(2, Z):
+            @pl.when(valid(t - d + 1) & (z + d < Z) & has_left)
+            def _():
+                key_here(t - d + 1, z + d, to_left).wait_recv()
+                key_here(t - d + 1, z + d, to_left).start()
+
+    reach = Z - 1
+    right_delay = z
+    left_delay = jnp.where(is_last, 0, 2 * reach - z)
+    last_delay = jnp.maximum(right_delay, left_delay)
+
+    @pl.loop(0, H + 2 * reach)
+    def _(t):
+        now = t
+
+        @pl.when(valid(now))
+        def _():
             @pl.when(has_left)
             def _():
-                halo_left(t).start()
-
-            arrive(0, t)
-
-            @pl.when(is_last)
-            def _():
-                query_left(t).start()
-
-        @pl.when(valid(t - 1) & has_right)
-        def _():
-            halo_left(t - 1).wait_recv()
-
-            @pl.when(has_left)
-            def _():
-                key_copy(ext.at[t - 1, :, F + W], t - 1, z + 1, to_left).start()
-
-        for d in range(1, Z - 1):
-            @pl.when(valid(t - d) & (z - d >= 0) & jnp.logical_not(is_last))
-            def _():
-                key_here(t - d, z - d, to_right).wait_recv()
-
-                @pl.when(keys_right)
-                def _():
-                    key_here(t - d, z - d, to_right).start()
-
-        for d in range(2, Z):
-            @pl.when(valid(t - d) & (z + d < Z))
-            def _():
-                key_here(t - d, z + d, to_left).wait_recv()
-
-                @pl.when(has_left)
-                def _():
-                    key_here(t - d, z + d, to_left).start()
-
-        now = t - delay
-
-        @pl.when(valid(now))
-        def _():
-            @pl.when(has_left)
-            def _():
                 halo_right(now).wait_recv()
 
+            @pl.when(is_first)
+            def _():
+                halo_left(now).wait_recv()
+                for g in range(2, Z):
+                    key_here(now, g, to_left).wait_recv()
+
             @pl.when(is_helper)
             def _():
                 query_left(now).wait_recv()
+                for g in range(Z - 2):
+                    key_here(now, g, to_right).wait_recv()
 
             @pl.when(is_last)
             def _():

time: 139 us -> 162 us (1.17)
  the two profiles are of different devices: /device:TPU:27 before, /device:TPU:0 now
where the time goes in v3:
time: 162 us; the launch traced here: 161 us
  Pallas kernels  159 us (98%)
  local copies, waits for them, and re-layouts  2.66 us (2%)
    pallas_call x1, Pallas kernels, shards(): pl.pallas_call(functools.partial(kernel, (F, S, H, SHARED, Z, W, NC)), ou...  159 us

profile of v3, /device:TPU:0, one launch (start us, length us, event | category | flops | bytes accessed | tf_op | source)
XLA Modules:
  0.0 161.5 jit_solution(11420114017548718306)
XLA Ops:
  0.0 158.8 %shard_map.73 = f32[4,64,1536]{2,1,0:T(8,128)} custom-call(s32[12]{0:T(128)} %win_ref.1, s32[12]{0:T(128)} %str_ref.1, s32[12]{0:T(128)} %cut_ref.1, f32[80]{0:T(128)} %constant.2.clone.basis_ref, f32[4,64,1536]{2,1,0:T(8,128)} %q_ref.1, f32[4,64,1536]{2,1,0:T(8,128)} %k_ref.1, f32[4,64,1536]{2,1,0:T(8,128)} %v_ref.1), custom_call_target="tpu_custom_call" | custom-call | tf_op jit(solution)/shard_map/pallas_call | solution.py:558
  158.8 2.7 %copy.9 = f32[4,64,1536]{2,1,0:T(8,128)} copy(f32[4,64,1536]{2,1,0:T(8,128)} %shard_map.73) | data formatting | bytes 3145728

commit v4 on v2

--- a/solution.py
+++ b/solution.py
@@ -168,13 +168,14 @@
             return j >= 0
         return jnp.where(half == 0, j < H - SHARED, j >= SHARED)
 
-    order = (1, 2, 0)
-
-    @pl.loop(0, H)
-    def _(j):
-        for which in order:
-            swap(which, j).start()
-            own_copy(which, j).start()
+    def fetch(which, j):
+        swap(which, j).start()
+        own_copy(which, j).start()
+
+    ahead = min(2, H)
+    for first in range(ahead):
+        for which in (1, 2, 0):
+            fetch(which, first)
 
     def zero_halo(first):
         @pl.loop(0, H)
@@ -302,9 +303,9 @@
         for i in range(F):
             edge[j, i] = expand(None, totals, at, i)
 
-    delay = jnp.where(is_last, 1, jnp.maximum(z, Z - 1 - z))
-    right_delay = Z - 1 + z
-    left_delay = jnp.where(is_last, 1, 2 * Z - 4 - z)
+    delay = jnp.where(is_last, 1, jnp.where(is_first | is_helper, Z - 2, jnp.maximum(z, Z - 1 - z)))
+    right_delay = jnp.where(is_last, 2 * Z - 2, Z - 2 + z)
+    left_delay = jnp.where(is_last, 2, Z - 1 + 2 * (Z - 2 - z))
     last_delay = jnp.maximum(right_delay, left_delay)
     from_first = z == 1
     middle_in_right = (z > 1) & (z < Z - 1)
@@ -315,13 +316,18 @@
     def valid(j):
         return (j >= 0) & (j < H)
 
-    @pl.loop(0, H + 2 * Z - 2)
+    @pl.loop(0, H + 3 * Z - 5)
     def _(t):
         @pl.when(t < H)
         def _():
             arrive(1, t)
             arrive(2, t)
 
+            @pl.when(t + ahead < H)
+            def _():
+                for which in (1, 2, 0):
+                    fetch(which, t + ahead)
+
             @pl.when(keys_right)
             def _():
                 key_copy(ext.at[t, :, W], t, z, to_right).start()
@@ -336,53 +342,83 @@
 
             arrive(0, t)
 
+        @pl.when(valid(t - 1) & is_last)
+        def _():
+            query_left(t - 1).start()
+
+        @pl.when(valid(t - 1) & has_right & has_left)
+        def _():
+            halo_left(t - 1).wait_recv()
+            key_copy(ext.at[t - 1, :, F + W], t - 1, z + 1, to_left).start()
+
+        for d in range(1, Z - 1):
+            @pl.when(valid(t - d) & (z - d >= 0) & keys_right)
+            def _():
+                key_here(t - d, z - d, to_right).wait_recv()
+                key_here(t - d, z - d, to_right).start()
+
+        for d in range(2, Z):
+            @pl.when(valid(t - d) & (z + d < Z) & has_left)
+            def _():
+                key_here(t - d, z + d, to_left).wait_recv()
+                key_here(t - d, z + d, to_left).start()
+
+        now = t - delay
+
+        @pl.when(valid(now))
+        def _():
+            @pl.when(has_left)
+            def _():
+                halo_right(now).wait_recv()
+
+            @pl.when(is_first)
+            def _():
+                halo_left(now).wait_recv()
+                for g in range(2, Z):
+                    key_here(now, g, to_left).wait_recv()
+
+            @pl.when(is_helper)
+            def _():
+                query_left(now).wait_recv()
+                for g in range(Z - 2):
+                    key_here(now, g, to_right).wait_recv()
+
             @pl.when(is_last)
             def _():
-                query_left(t).start()
-
-        @pl.when(valid(t - 1) & has_right)
-        def _():
-            halo_left(t - 1).wait_recv()
-
-            @pl.when(has_left)
-            def _():
-                key_copy(ext.at[t - 1, :, F + W], t - 1, z + 1, to_left).start()
-
-        for d in range(1, Z - 1):
-            @pl.when(valid(t - d) & (z - d >= 0) & jnp.logical_not(is_last))
-            def _():
-                key_here(t - d, z - d, to_right).wait_recv()
-
-                @pl.when(keys_right)
-                def _():
-                    key_here(t - d, z - d, to_right).start()
-
-        for d in range(2, Z):
-            @pl.when(valid(t - d) & (z + d < Z))
-            def _():
-                key_here(t - d, z + d, to_left).wait_recv()
-
-                @pl.when(has_left)
-                def _():
-                    key_here(t - d, z + d, to_left).start()
-
-        now = t - delay
-
-        @pl.when(valid(now))
-        def _():
-            @pl.when(has_left)
-            def _():
-                halo_right(now).wait_recv()
+                query_left(now).wait_send()
+
+            compute(now)
+
+        jl = t - left_delay
+
+        @pl.when(valid(jl))
+        def _():
+            @pl.when(is_last)
+            def _():
+                sum_left_first(jl).start()
 
             @pl.when(is_helper)
             def _():
-                query_left(now).wait_recv()
-
-            @pl.when(is_last)
-            def _():
-                query_left(now).wait_send()
-
-            compute(now)
+                sum_left_first(jl).wait_recv()
+                add_raw(lsum, jl, Z - 1)
+
+            @pl.when(middle_in_left)
+            def _():
+                sum_left_full(jl).wait_recv()
+                lsum[jl] = lsum[jl] + coef[jl]
+
+            @pl.when(is_first)
+            def _():
+                sum_left_last(jl).wait_recv()
+
+            @pl.when(middle_out_left)
+            def _():
+                sum_left_full(jl).start()
+
+            @pl.when(from_first)
+            def _():
+                fill_edge(edge_l, lsum, jl, 0)
+                sum_left_last(jl).start()
 
         jr = t - right_delay
 
@@ -414,37 +450,6 @@
             def _():
                 fill_edge(edge_r, rsum, jr, Z - 1)
                 sum_right_last(jr).start()
-
-        jl = t - left_delay
-
-        @pl.when(valid(jl))
-        def _():
-            @pl.when(is_last)
-            def _():
-                sum_left_first(jl).start()
-
-            @pl.when(is_helper)
-            def _():
-                sum_left_first(jl).wait_recv()
-                add_raw(lsum, jl, Z - 1)
-
-            @pl.when(middle_in_left)
-            def _():
-                sum_left_full(jl).wait_recv()
-                lsum[jl] = lsum[jl] + coef[jl]
-
-            @pl.when(is_first)
-            def _():
-                sum_left_last(jl).wait_recv()
-
-            @pl.when(middle_out_left)
-            def _():
-                sum_left_full(jl).start()
-
-            @pl.when(from_first)
-            def _():
-                fill_edge(edge_l, lsum, jl, 0)
-                sum_left_last(jl).start()
 
         jf = t - last_delay
 

time: 139 us -> 139 us (level)
  the two profiles are of different devices: /device:TPU:27 before, /device:TPU:0 now
where the time goes in v4:
time: 139 us
  Pallas kernels  136 us (98%)
  local copies, waits for them, and re-layouts  2.66 us (2%)
    pallas_call x1, Pallas kernels, shards(): pl.pallas_call(functools.partial(kernel, (F, S, H, SHARED, Z, W, NC)), ou...  136 us

profile of v4, /device:TPU:0, one launch (start us, length us, event | category | flops | bytes accessed | tf_op | source)
XLA Modules:
  0.0 138.8 jit_solution(2674295112853202059)
XLA Ops:
  0.0 136.2 %shard_map.73 = f32[4,64,1536]{2,1,0:T(8,128)} custom-call(s32[12]{0:T(128)} %win_ref.1, s32[12]{0:T(128)} %str_ref.1, s32[12]{0:T(128)} %cut_ref.1, f32[80]{0:T(128)} %constant.2.clone.basis_ref, f32[4,64,1536]{2,1,0:T(8,128)} %q_ref.1, f32[4,64,1536]{2,1,0:T(8,128)} %k_ref.1, f32[4,64,1536]{2,1,0:T(8,128)} %v_ref.1), custom_call_target="tpu_custom_call" | custom-call | tf_op jit(solution)/shard_map/pallas_call | solution.py:549
  136.2 2.7 %copy.9 = f32[4,64,1536]{2,1,0:T(8,128)} copy(f32[4,64,1536]{2,1,0:T(8,128)} %shard_map.73) | data formatting | bytes 3145728

commit v5 on v4

--- a/solution.py
+++ b/solution.py
@@ -21,15 +21,18 @@
     return high, low
 
 
-def soft_rows(q_wide, keys, values, bias):
-    rows = q_wide.shape[0]
-    scores = lax.dot_general(
-        q_wide, keys, (((1,), (1,)), ((), ())), preferred_element_type=jnp.float32
-    )
+def score_rows(q_wide, keys):
+    return jnp.dot(q_wide, keys, preferred_element_type=jnp.float32)
+
+
+def soft(scores, bias):
     scores = scores + bias
-    highest = jnp.max(scores, axis=1, keepdims=True)
-    weights = jnp.exp(scores - highest)
-    total = jnp.sum(weights, axis=1, keepdims=True)
+    weights = jnp.exp2(scores - jnp.max(scores, axis=1, keepdims=True))
+    return weights, jnp.sum(weights, axis=1, keepdims=True)
+
+
+def weigh(weights, total, values):
+    rows = weights.shape[0]
     both = jnp.concatenate(split_two(weights), axis=0)
     wide = jnp.dot(both, values, preferred_element_type=jnp.float32)
     summed = (wide[:rows, :DH] + wide[:rows, DH:]) + (wide[rows:, :DH] + wide[rows:, DH:])
@@ -37,13 +40,13 @@
 
 
 def fill_split(key, value, keys_wide, values_wide, row, count):
-    kh, kl = split_two(key)
+    kh, kl = split_two(key.T)
     vh, vl = split_two(value)
     rows = pl.ds(row, count)
-    keys_wide[rows, 0:DH] = kh
-    keys_wide[rows, DH : 2 * DH] = kh
-    keys_wide[rows, 2 * DH : 3 * DH] = kl
-    keys_wide[rows, 3 * DH : 4 * DH] = kl
+    keys_wide[0:DH, rows] = kh
+    keys_wide[DH : 2 * DH, rows] = kh
+    keys_wide[2 * DH : 3 * DH, rows] = kl
+    keys_wide[3 * DH : 4 * DH, rows] = kl
     values_wide[rows, 0:DH] = vh
     values_wide[rows, DH : 2 * DH] = vl
 
@@ -207,8 +210,36 @@
             )
 
         def wide_query(i):
-            qh, ql = split_two(rowbuf[j, i] * (DH**-0.5))
+            both = rowbuf[j, pl.ds(i, 2)].reshape(2 * TOK, DH)
+            qh, ql = split_two(both * (DH**-0.5 * math.log2(math.e)))
             return jnp.concatenate([qh, ql, qh, ql], axis=1)
+
+        def near_pair(i, q_wide):
+            span = (2 * W + 1) * TOK
+            rows = pl.ds(i * TOK, span + TOK)
+            scores = score_rows(q_wide, ks[:, rows])
+            parts, totals = [], []
+            for u in range(2):
+                flags = []
+                for off in range(-W, W + 1):
+                    frame = z * F + i + u + off
+                    flags.append((abs(off) <= window) & (frame >= 0) & (frame < Z * F))
+                part = scores[u * TOK : (u + 1) * TOK, u * TOK : u * TOK + span]
+                weights, total = soft(part, bias_row(flags))
+                empty = jnp.zeros((TOK, TOK), jnp.float32)
+                pieces = [weights, empty] if u == 0 else [empty, weights]
+                parts.append(jnp.concatenate(pieces, axis=1))
+                totals.append(total)
+            return weigh(jnp.concatenate(parts, axis=0), jnp.concatenate(totals, axis=0), vs[rows])
+
+        def far_pair(q_wide, far_bias):
+            weights, total = soft(score_rows(q_wide, kgs[...]), far_bias)
+            return weigh(weights, total, vgs[...])
+
+        def keep_pair(i, local, wide):
+            local = local.reshape(2, TOK, DH)
+            rowbuf[j, i : i + 2] = local
+            dbuf[i : i + 2] = -local if wide is None else wide.reshape(2, TOK, DH) - local
 
         @pl.when(jnp.logical_not(is_last))
         def _():
@@ -217,24 +248,21 @@
             for g in range(Z):
                 fill_split(far[j, 0, g], far[j, 1, g], kgs, vgs, g * TOK, TOK)
             far_bias = bias_row([((g * KSTRIDE) & (stride - 1)) == 0 for g in range(Z)])
-
-            @pl.loop(0, jnp.where(is_helper, 2 * F, F))
-            def _(i):
-                dbuf[i] = soft_rows(wide_query(i), kgs[...], vgs[...], far_bias)
+            for i in range(0, F, 2):
+                q_wide = wide_query(i)
+                keep_pair(i, near_pair(i, q_wide), far_pair(q_wide, far_bias))
+
+            @pl.when(is_helper)
+            def _():
+                for i in range(F, 2 * F, 2):
+                    wide = far_pair(wide_query(i), far_bias)
+                    dbuf[i : i + 2] = wide.reshape(2, TOK, DH)
 
         @pl.when(is_last)
         def _():
-            dbuf[0:F] = jnp.zeros((F, TOK, DH), jnp.float32)
-
-        for i in range(F):
-            flags = []
-            for off in range(-W, W + 1):
-                frame = z * F + i + off
-                flags.append((abs(off) <= window) & (frame >= 0) & (frame < Z * F))
-            near_rows = pl.ds(i * TOK, (2 * W + 1) * TOK)
-            local = soft_rows(wide_query(i), ks[near_rows], vs[near_rows], bias_row(flags))
-            rowbuf[j, i] = local
-            dbuf[i] = dbuf[i] - local
+            for i in range(0, F, 2):
+                keep_pair(i, near_pair(i, wide_query(i)), None)
+
         for c in range(NC):
             coef[j, c] = keep_of(j, c) * project([dbuf[i] for i in range(F)], z, c)
 
@@ -561,9 +589,9 @@
             pltpu.VMEM((H, F, TOK, DH), f32),
             pltpu.VMEM((H, F, TOK, DH), f32),
             pltpu.VMEM((2 * F, TOK, DH), f32),
-            pltpu.VMEM(((F + 2 * W) * TOK, 4 * DH), bf16),
+            pltpu.VMEM((4 * DH, (F + 2 * W) * TOK), bf16),
             pltpu.VMEM(((F + 2 * W) * TOK, 2 * DH), bf16),
-            pltpu.VMEM((Z * TOK, 4 * DH), bf16),
+            pltpu.VMEM((4 * DH, Z * TOK), bf16),
             pltpu.VMEM((Z * TOK, 2 * DH), bf16),
             dma((3, H)), dma((3, H)), dma((3, H)),
             dma((H,)), dma((H,)), dma((H,)), dma((H,)),

time: 139 us -> 135 us (0.971)
  Pallas kernels: 136 us -> 132 us
    pallas_call x1, Pallas kernels: 136 us -> 132 us  [shards(): pl.pallas_call(functools.partial(kernel, (F, S, H, SHARED, Z, W, NC)), ou...]
where the time goes in v5:
time: 135 us
  Pallas kernels  132 us (98%)
  local copies, waits for them, and re-layouts  2.66 us (2%)
    pallas_call x1, Pallas kernels, shards(): pl.pallas_call(functools.partial(kernel, (F, S, H, SHARED, Z, W, NC)), ou...  132 us

profile of v5, /device:TPU:0, one launch (start us, length us, event | category | flops | bytes accessed | tf_op | source)
XLA Modules:
  0.0 135.1 jit_solution(11611634886436623188)
XLA Ops:
  0.0 132.4 %shard_map.73 = f32[4,64,1536]{2,1,0:T(8,128)} custom-call(s32[12]{0:T(128)} %win_ref.1, s32[12]{0:T(128)} %str_ref.1, s32[12]{0:T(128)} %cut_ref.1, f32[80]{0:T(128)} %constant.2.clone.basis_ref, f32[4,64,1536]{2,1,0:T(8,128)} %q_ref.1, f32[4,64,1536]{2,1,0:T(8,128)} %k_ref.1, f32[4,64,1536]{2,1,0:T(8,128)} %v_ref.1), custom_call_target="tpu_custom_call" | custom-call | tf_op jit(solution)/shard_map/pallas_call | solution.py:577
  132.4 2.7 %copy.9 = f32[4,64,1536]{2,1,0:T(8,128)} copy(f32[4,64,1536]{2,1,0:T(8,128)} %shard_map.73) | data formatting | bytes 3145728

commit v6 on v5

--- a/solution.py
+++ b/solution.py
@@ -70,7 +70,11 @@
     is_first = z == 0
     is_last = z == Z - 1
     is_helper = z == Z - 2
-    keys_right = z < Z - 2
+    HH = H // 2
+
+    def keys_right(j):
+        return (z < Z - 2) | (is_helper & (j >= HH))
+
     to_right, to_left, to_other = {"frm": right}, {"frm": left}, {"pos": other}
 
     def remote(src, dst, send, recv, to):
@@ -241,10 +245,16 @@
             rowbuf[j, i : i + 2] = local
             dbuf[i : i + 2] = -local if wide is None else wide.reshape(2, TOK, DH) - local
 
-        @pl.when(jnp.logical_not(is_last))
+        no_far = is_last & (j < HH)
+
+        @pl.when(jnp.logical_not(no_far))
         def _():
             far[j, :, z] = ext[j, :, W]
-            far[j, :, z + 1] = ext[j, :, F + W]
+
+            @pl.when(has_right)
+            def _():
+                far[j, :, z + 1] = ext[j, :, F + W]
+
             for g in range(Z):
                 fill_split(far[j, 0, g], far[j, 1, g], kgs, vgs, g * TOK, TOK)
             far_bias = bias_row([((g * KSTRIDE) & (stride - 1)) == 0 for g in range(Z)])
@@ -252,13 +262,13 @@
                 q_wide = wide_query(i)
                 keep_pair(i, near_pair(i, q_wide), far_pair(q_wide, far_bias))
 
-            @pl.when(is_helper)
+            @pl.when(is_helper & (j < HH))
             def _():
                 for i in range(F, 2 * F, 2):
                     wide = far_pair(wide_query(i), far_bias)
                     dbuf[i : i + 2] = wide.reshape(2, TOK, DH)
 
-        @pl.when(is_last)
+        @pl.when(no_far)
         def _():
             for i in range(0, F, 2):
                 keep_pair(i, near_pair(i, wide_query(i)), None)
@@ -266,7 +276,7 @@
         for c in range(NC):
             coef[j, c] = keep_of(j, c) * project([dbuf[i] for i in range(F)], z, c)
 
-        @pl.when(is_helper)
+        @pl.when(is_helper & (j < HH))
         def _():
             for c in range(NC):
                 more = project([dbuf[F + i] for i in range(F)], Z - 1, c)
@@ -331,9 +341,9 @@
         for i in range(F):
             edge[j, i] = expand(None, totals, at, i)
 
-    delay = jnp.where(is_last, 1, jnp.where(is_first | is_helper, Z - 2, jnp.maximum(z, Z - 1 - z)))
-    right_delay = jnp.where(is_last, 2 * Z - 2, Z - 2 + z)
-    left_delay = jnp.where(is_last, 2, Z - 1 + 2 * (Z - 2 - z))
+    delay = jnp.where(is_first | is_last | is_helper, Z - 2, jnp.maximum(z, Z - 1 - z))
+    right_delay = Z - 2 + 2 * z
+    left_delay = jnp.where(is_last, Z - 2, jnp.where(is_first, 2 * Z, 2 * Z - 2 - z))
     last_delay = jnp.maximum(right_delay, left_delay)
     from_first = z == 1
     middle_in_right = (z > 1) & (z < Z - 1)
@@ -344,7 +354,7 @@
     def valid(j):
         return (j >= 0) & (j < H)
 
-    @pl.loop(0, H + 3 * Z - 5)
+    @pl.loop(0, H + max(2 * Z, 3 * Z - 4))
     def _(t):
         @pl.when(t < H)
         def _():
@@ -356,7 +366,7 @@
                 for which in (1, 2, 0):
                     fetch(which, t + ahead)
 
-            @pl.when(keys_right)
+            @pl.when(keys_right(t))
             def _():
                 key_copy(ext.at[t, :, W], t, z, to_right).start()
 
@@ -370,7 +380,7 @@
 
             arrive(0, t)
 
-        @pl.when(valid(t - 1) & is_last)
+        @pl.when(valid(t - 1) & is_last & (t - 1 < HH))
         def _():
             query_left(t - 1).start()
 
@@ -380,7 +390,7 @@
             key_copy(ext.at[t - 1, :, F + W], t - 1, z + 1, to_left).start()
 
         for d in range(1, Z - 1):
-            @pl.when(valid(t - d) & (z - d >= 0) & keys_right)
+            @pl.when(valid(t - d) & (z - d >= 0) & keys_right(t - d))
             def _():
                 key_here(t - d, z - d, to_right).wait_recv()
                 key_here(t - d, z - d, to_right).start()
@@ -405,17 +415,53 @@
                 for g in range(2, Z):
                     key_here(now, g, to_left).wait_recv()
 
-            @pl.when(is_helper)
+            @pl.when(is_helper & (now < HH))
             def _():
                 query_left(now).wait_recv()
                 for g in range(Z - 2):
                     key_here(now, g, to_right).wait_recv()
 
+            @pl.when(is_last & (now < HH))
+            def _():
+                query_left(now).wait_send()
+
+            @pl.when(is_last & (now >= HH))
+            def _():
+                for g in range(Z - 1):
+                    key_here(now, g, to_right).wait_recv()
+
+            compute(now)
+
+        jr = t - right_delay
+
+        @pl.when(valid(jr))
+        def _():
+            @pl.when(is_first)
+            def _():
+                sum_right_first(jr).start()
+
+            @pl.when(from_first)
+            def _():
+                sum_right_first(jr).wait_recv()
+                add_raw(rsum, jr, 0)
+
+            @pl.when(middle_in_right)
+            def _():
+                sum_right_full(jr).wait_recv()
+                rsum[jr] = rsum[jr] + coef[jr]
+
             @pl.when(is_last)
             def _():
-                query_left(now).wait_send()
-
-            compute(now)
+                sum_right_last(jr).wait_recv()
+
+            @pl.when(middle_out_right)
+            def _():
+                sum_right_full(jr).start()
+
+            @pl.when(is_helper)
+            def _():
+                fill_edge(edge_r, rsum, jr, Z - 1)
+                sum_right_last(jr).start()
 
         jl = t - left_delay
 
@@ -447,37 +493,6 @@
             def _():
                 fill_edge(edge_l, lsum, jl, 0)
                 sum_left_last(jl).start()
-
-        jr = t - right_delay
-
-        @pl.when(valid(jr))
-        def _():
-            @pl.when(is_first)
-            def _():
-                sum_right_first(jr).start()
-
-            @pl.when(from_first)
-            def _():
-                sum_right_first(jr).wait_recv()
-                add_raw(rsum, jr, 0)
-
-            @pl.when(middle_in_right)
-            def _():
-                sum_right_full(jr).wait_recv()
-                rsum[jr] = rsum[jr] + coef[jr]
-
-            @pl.when(is_last)
-            def _():
-                sum_right_last(jr).wait_recv()
-
-            @pl.when(middle_out_right)
-            def _():
-                sum_right_full(jr).start()
-
-            @pl.when(is_helper)
-            def _():
-                fill_edge(edge_r, rsum, jr, Z - 1)
-                sum_right_last(jr).start()
 
         jf = t - last_delay
 
@@ -490,7 +505,7 @@
         for which in range(3):
             swap(which, j).wait_send()
 
-        @pl.when(keys_right)
+        @pl.when(keys_right(j))
         def _():
             key_copy(ext.at[j, :, W], j, z, to_right).wait_send()
 
@@ -531,7 +546,7 @@
             key_copy(ext.at[j, :, F + W], j, z + 1, to_left).wait_send()
 
         for d in range(1, Z - 1):
-            @pl.when((z - d >= 0) & keys_right)
+            @pl.when((z - d >= 0) & keys_right(j))
             def _():
                 key_here(j, z - d, to_right).wait_send()
 

time: 135 us -> 128 us (0.948)
  Pallas kernels: 132 us -> 126 us
    pallas_call x1, Pallas kernels: 132 us -> 126 us  [shards(): pl.pallas_call(functools.partial(kernel, (F, S, H, SHARED, Z, W, NC)), ou...]
where the time goes in v6:
time: 128 us
  Pallas kernels  126 us (98%)
  local copies, waits for them, and re-layouts  2.66 us (2%)
    pallas_call x1, Pallas kernels, shards(): pl.pallas_call(functools.partial(kernel, (F, S, H, SHARED, Z, W, NC)), ou...  126 us
    unnamed x1, local copies, waits for them, and re-layouts  2.66 us

profile of v6, /device:TPU:0, one launch (start us, length us, event | category | flops | bytes accessed | tf_op | source)
XLA Modules:
  0.0 128.3 jit_solution(7073723548815955728)
XLA Ops:
  0.0 125.6 %shard_map.73 = f32[4,64,1536]{2,1,0:T(8,128)} custom-call(s32[12]{0:T(128)} %win_ref.1, s32[12]{0:T(128)} %str_ref.1, s32[12]{0:T(128)} %cut_ref.1, f32[80]{0:T(128)} %constant.2.clone.basis_ref, f32[4,64,1536]{2,1,0:T(8,128)} %q_ref.1, f32[4,64,1536]{2,1,0:T(8,128)} %k_ref.1, f32[4,64,1536]{2,1,0:T(8,128)} %v_ref.1), custom_call_target="tpu_custom_call" | custom-call | tf_op jit(solution)/shard_map/pallas_call | solution.py:592
  125.7 2.7 %copy.9 = f32[4,64,1536]{2,1,0:T(8,128)} copy(f32[4,64,1536]{2,1,0:T(8,128)} %shard_map.73) | data formatting | bytes 3145728
